TPU v7x, 128 devices: a whole 4x4x4 slice. The times are simulated.
128 devices in a mesh: dp: 32 (over y, z, core), tensor: 4 (over x).
Axes of the slice: x: 4, y: 4, z: 4, core: 2. Of those that a mesh axis runs over, the one named last changes fastest.
Arguments:
- block_input: float32 [32768, 768], P('dp'), may hold values from -6 to 6
- lengths: int32 [32], P('dp'), may hold values from 1 to 1024, 22528 in all
- cotangent: float32 [32768, 768], P('dp'), may hold values from -6 to 6
- w_query: bfloat16 [2, 768, 768], P(None, None, 'tensor'), may hold values from -0.21875 to 0.21875
- w_key: bfloat16 [2, 768, 768], P(None, None, 'tensor'), may hold values from -0.21875 to 0.21875
- w_value: bfloat16 [2, 768, 768], P(None, None, 'tensor'), may hold values from -0.21875 to 0.21875
- w_output: bfloat16 [2, 768, 768], P(None, 'tensor'), may hold values from -3 to 3
- w_gate: bfloat16 [2, 768, 2048], P(None, None, 'tensor'), may hold values from -0.21875 to 0.21875
- w_up: bfloat16 [2, 768, 2048], P(None, None, 'tensor'), may hold values from -0.21875 to 0.21875
- w_down: bfloat16 [2, 2048, 768], P(None, 'tensor'), may hold values from -0.125 to 0.125
- gains: float32 [4, 768], replicated, may hold values from 0.5 to 1.5
Outputs:
- block_output: float32 [32768, 768], P('dp')
- input_grad: float32 [32768, 768], P('dp')
- query_grad: float32 [2, 768, 768], P(None, 'dp', 'tensor')
- key_grad: float32 [2, 768, 768], P(None, 'dp', 'tensor')
- value_grad: float32 [2, 768, 768], P(None, 'dp', 'tensor')
- output_grad: float32 [2, 768, 768], P(None, 'tensor', 'dp')
- gate_grad: float32 [2, 768, 2048], P(None, 'dp', 'tensor')
- up_grad: float32 [2, 768, 2048], P(None, 'dp', 'tensor')
- down_grad: float32 [2, 2048, 768], P(None, 'tensor', 'dp')
- gain_grads: float32 [3, 768], P(None, 'dp')
- ffn_gain_grad: float32 [768], P('dp')
Inputs may be any that keep to these rules, and one draw needn't show every extreme that they name: The 32 lengths sum to 22528, and the longest is exactly 1024.
All inputs are finite; a program needn't handle non-finite values. No bound on the sum of `lengths` on one device may be relied on, other than what follows from the above.
Results may differ from a plain program's by a relative error of at most 0.025.
The roundings to bfloat16 on the way count: a program that leaves them out, or rounds other values in their place, can miss the bound.
Values sent between devices are 32-bit elements; how exact they have to be, the bound alone decides.
A program may use at most 256 MiB of HBM per device.

v0:
```python
import jax
import jax.numpy as jnp
from jax import lax
from jax.sharding import PartitionSpec as P

HEAD_DIM = 64


negative = -1e30
epsilon = 1e-05


def split_up(value, dim, peers):
    shape = value.shape
    blocks = value.reshape(*shape[:dim], peers, shape[dim] // peers, *shape[dim + 1 :])
    return jnp.moveaxis(blocks, dim, 0)


def sum_packed(arrays, axis, dims):
    peers = lax.axis_size(axis)
    blocks = [split_up(a, dim, peers) for a, dim in zip(arrays, dims)]
    lines = jnp.concatenate([b.reshape(peers, -1) for b in blocks], axis=1)
    extent = max(16, -(-lines.shape[1] // 1024) * 8)
    lines = jnp.pad(lines, ((0, 0), (0, extent * 128 - lines.shape[1]))).reshape(-1, 128)
    line, at, finished = (lax.psum_scatter(lines, axis, tiled=True).reshape(-1), 0, [])
    for b in blocks:
        part = b[0]
        finished.append(line[at : at + part.size].reshape(part.shape))
        at += part.size
    return tuple(finished)


def rope_tables(count):
    half = HEAD_DIM // 2
    freq = 10000.0 ** (-jnp.arange(half, dtype=jnp.float32) * 2.0 / HEAD_DIM)
    angle = jnp.arange(count, dtype=jnp.float32)[:, None] * freq[None, :]
    cosine = jnp.concatenate([jnp.cos(angle), jnp.cos(angle)], axis=1)
    sine = jnp.concatenate([jnp.sin(angle), jnp.sin(angle)], axis=1)
    return (cosine[:, None, :], sine[:, None, :])


def rotate(values, cosine, sine):
    half = HEAD_DIM // 2
    turned = jnp.concatenate([-values[..., half:], values[..., :half]], axis=-1)
    return values * cosine + turned * sine


def unrotate(grads, cosine, sine):
    half = HEAD_DIM // 2
    scaled = grads * sine
    back = jnp.concatenate([scaled[..., half:], -scaled[..., :half]], axis=-1)
    return grads * cosine + back


def norm_forward(resid, gain):
    factor = lax.rsqrt(jnp.mean(resid * resid, axis=-1, keepdims=True) + epsilon)
    normed = resid * factor
    return (normed * gain, normed, factor)


def norm_backward(grad, normed, factor, gain):
    gain_grad = jnp.sum(grad * normed, axis=0)
    inner = grad * gain
    return (factor * (inner - normed * jnp.mean(inner * normed, axis=-1, keepdims=True)), gain_grad)


def branch_total(part):
    return lax.psum(part, "tensor")


def input_total(part):
    return lax.psum(part, "tensor")


def score_block(queries, keys, length):
    count = queries.shape[0]
    raw = jnp.einsum(
        "shd,thd->hst", queries, keys, preferred_element_type=jnp.float32
    ) * HEAD_DIM ** (-0.5)
    rows = jnp.arange(count, dtype=jnp.int32)[:, None]
    cols = jnp.arange(count, dtype=jnp.int32)[None, :]
    allowed = (cols <= rows) & (cols < length)
    return jnp.where(allowed[None], raw, negative)


def outer_sum(left, right):
    return jnp.einsum("sa,sb->ab", left, right, preferred_element_type=jnp.float32)


def back_product(grad, weight):
    return jnp.einsum("sb,ab->sa", grad, weight, preferred_element_type=jnp.float32)


def attend_forward(inputs, w_q, w_k, w_v, w_o, cosine, sine, length):
    count = inputs.shape[0]
    heads = w_q.shape[1] // HEAD_DIM

    def project(weight):
        return jnp.dot(inputs, weight, preferred_element_type=jnp.float32).reshape(
            count, heads, HEAD_DIM
        )

    queries = rotate(project(w_q), cosine, sine).astype(jnp.bfloat16)
    keys = rotate(project(w_k), cosine, sine).astype(jnp.bfloat16)
    values = project(w_v).astype(jnp.bfloat16)
    scores = score_block(queries, keys, length)
    peak = jnp.max(scores, axis=-1, keepdims=True)
    logsum = peak + jnp.log(jnp.sum(jnp.exp(scores - peak), axis=-1, keepdims=True))
    probs = jnp.exp(scores - logsum).astype(jnp.bfloat16)
    mixed = jnp.einsum("hst,thd->shd", probs, values, preferred_element_type=jnp.float32)
    mixed = mixed.reshape(count, heads * HEAD_DIM).astype(jnp.bfloat16)
    part = jnp.dot(mixed, w_o, preferred_element_type=jnp.float32)
    return (part, (inputs, queries, keys, values, mixed, logsum))


def attend_backward(grad, saved, w_q, w_k, w_v, w_o, cosine, sine, length):
    inputs, queries, keys, values, mixed, logsum = saved
    count = inputs.shape[0]
    heads = w_q.shape[1] // HEAD_DIM
    grad_low = grad.astype(jnp.bfloat16)
    grad_wo = outer_sum(mixed, grad_low)
    grad_mixed = back_product(grad_low, w_o).reshape(count, heads, HEAD_DIM).astype(jnp.bfloat16)
    probs = jnp.exp(score_block(queries, keys, length) - logsum)
    grad_probs = jnp.einsum("shd,thd->hst", grad_mixed, values, preferred_element_type=jnp.float32)
    inner = jnp.sum(probs * grad_probs, axis=-1, keepdims=True)
    grad_scores = (probs * (grad_probs - inner)).astype(jnp.bfloat16)
    grad_values = jnp.einsum(
        "hst,shd->thd", probs.astype(jnp.bfloat16), grad_mixed, preferred_element_type=jnp.float32
    )
    grad_values = grad_values.reshape(count, heads * HEAD_DIM).astype(jnp.bfloat16)
    grad_rq = jnp.einsum(
        "hst,thd->shd", grad_scores, keys, preferred_element_type=jnp.float32
    ) * HEAD_DIM ** (-0.5)
    grad_rk = jnp.einsum(
        "hst,shd->thd", grad_scores, queries, preferred_element_type=jnp.float32
    ) * HEAD_DIM ** (-0.5)
    grad_queries = (
        unrotate(grad_rq, cosine, sine).reshape(count, heads * HEAD_DIM).astype(jnp.bfloat16)
    )
    grad_keys = (
        unrotate(grad_rk, cosine, sine).reshape(count, heads * HEAD_DIM).astype(jnp.bfloat16)
    )
    grad_wq = outer_sum(inputs, grad_queries)
    grad_wk = outer_sum(inputs, grad_keys)
    grad_wv = outer_sum(inputs, grad_values)
    partial_value = (
        back_product(grad_queries, w_q)
        + back_product(grad_keys, w_k)
        + back_product(grad_values, w_v)
    )
    return (partial_value, (grad_wq, grad_wk, grad_wv, grad_wo))


def feed_forward(inputs, w_g, w_u, w_d):
    gate = jnp.dot(inputs, w_g, preferred_element_type=jnp.float32)
    up_val = jnp.dot(inputs, w_u, preferred_element_type=jnp.float32)
    hidden = (jax.nn.silu(gate) * up_val).astype(jnp.bfloat16)
    part = jnp.dot(hidden, w_d, preferred_element_type=jnp.float32)
    return (part, (inputs, gate, up_val, hidden))


def feed_backward(grad, saved, w_g, w_u, w_d):
    inputs, gate, up_val, hidden = saved
    grad_low = grad.astype(jnp.bfloat16)
    grad_wd = outer_sum(hidden, grad_low)
    grad_hidden = back_product(grad_low, w_d)
    sigma = jax.nn.sigmoid(gate)
    grad_gate = (grad_hidden * up_val * sigma * (1.0 + gate * (1.0 - sigma))).astype(jnp.bfloat16)
    grad_up = (grad_hidden * jax.nn.silu(gate)).astype(jnp.bfloat16)
    grad_wg = outer_sum(inputs, grad_gate)
    grad_wu = outer_sum(inputs, grad_up)
    partial_value = back_product(grad_gate, w_g) + back_product(grad_up, w_u)
    return (partial_value, (grad_wg, grad_wu, grad_wd))


def local(
    block_input, lengths, cotangent, w_query, w_key, w_value, w_output, w_gate, w_up, w_down, gains
):
    count = block_input.shape[0]
    length = lengths[0]
    cosine, sine = rope_tables(count)
    live = (jnp.arange(count, dtype=jnp.int32) < length).astype(jnp.float32)[:, None]
    part, attn0 = attend_forward(
        block_input.astype(jnp.bfloat16),
        w_query[0],
        w_key[0],
        w_value[0],
        w_output[0],
        cosine,
        sine,
        length,
    )
    hidden_state, normed1, factor1 = norm_forward(block_input + branch_total(part), gains[0])
    part, ffn0 = feed_forward(hidden_state.astype(jnp.bfloat16), w_gate[0], w_up[0], w_down[0])
    layer_out, normed2, factor2 = norm_forward(hidden_state + branch_total(part), gains[1])
    pre_attn, normed3, factor3 = norm_forward(layer_out, gains[2])
    part, attn1 = attend_forward(
        pre_attn.astype(jnp.bfloat16),
        w_query[1],
        w_key[1],
        w_value[1],
        w_output[1],
        cosine,
        sine,
        length,
    )
    middle = layer_out + branch_total(part)
    pre_ffn, normed4, factor4 = norm_forward(middle, gains[3])
    part, ffn1 = feed_forward(pre_ffn.astype(jnp.bfloat16), w_gate[1], w_up[1], w_down[1])
    block_output = (middle + branch_total(part)) * live
    grad_final = cotangent * live
    part, ffn1_grads = feed_backward(grad_final, ffn1, w_gate[1], w_up[1], w_down[1])
    grad_mid_norm, gain3 = norm_backward(input_total(part), normed4, factor4, gains[3])
    grad_middle = grad_final + grad_mid_norm
    part, attn1_grads = attend_backward(
        grad_middle, attn1, w_query[1], w_key[1], w_value[1], w_output[1], cosine, sine, length
    )
    grad_out_norm, gain2 = norm_backward(input_total(part), normed3, factor3, gains[2])
    grad_layer_out = grad_middle + grad_out_norm
    grad_resid2, gain1 = norm_backward(grad_layer_out, normed2, factor2, gains[1])
    part, ffn0_grads = feed_backward(grad_resid2, ffn0, w_gate[0], w_up[0], w_down[0])
    grad_hidden = grad_resid2 + input_total(part)
    grad_resid1, gain0 = norm_backward(grad_hidden, normed1, factor1, gains[0])
    part, attn0_grads = attend_backward(
        grad_resid1, attn0, w_query[0], w_key[0], w_value[0], w_output[0], cosine, sine, length
    )
    input_grad = grad_resid1 + input_total(part)
    stacked = [jnp.stack([attn0_grads[index], attn1_grads[index]]) for index in range(4)]
    stacked = stacked + [jnp.stack([ffn0_grads[index], ffn1_grads[index]]) for index in range(3)]
    total = sum_packed(
        (
            stacked[0],
            stacked[1],
            stacked[2],
            stacked[3],
            stacked[4],
            stacked[5],
            stacked[6],
            jnp.stack([gain0, gain1, gain2, gain3]),
        ),
        "dp",
        (1, 1, 1, 2, 1, 1, 2, 1),
    )
    summed = [total[index] for index in range(7)]
    gain_grads = total[7][:3]
    ffn_gain_grad = total[7][3]
    return (
        block_output,
        input_grad,
        summed[0],
        summed[1],
        summed[2],
        summed[3],
        summed[4],
        summed[5],
        summed[6],
        gain_grads,
        ffn_gain_grad,
    )


def solution(mesh):
    return jax.shard_map(
        local,
        mesh=mesh,
        in_specs=(
            P("dp", None),
            P("dp"),
            P("dp", None),
            P(None, None, "tensor"),
            P(None, None, "tensor"),
            P(None, None, "tensor"),
            P(None, "tensor", None),
            P(None, None, "tensor"),
            P(None, None, "tensor"),
            P(None, "tensor", None),
            P(),
        ),
        out_specs=(
            P("dp", None),
            P("dp", None),
            P(None, "dp", "tensor"),
            P(None, "dp", "tensor"),
            P(None, "dp", "tensor"),
            P(None, "tensor", "dp"),
            P(None, "dp", "tensor"),
            P(None, "dp", "tensor"),
            P(None, "tensor", "dp"),
            P(None, "dp"),
            P("dp"),
        ),
        check_vma=False,
    )
```

profile of v0, /device:TPU:1, one launch (start us, length us, event | category | flops | bytes accessed | tf_op | source)
XLA Modules:
  0.0 969.5 jit_solution(322292381929535122)
XLA Ops:
  18.1 4.4 exponential_reduce_fusion.1
  33.9 78.4 %all-reduce.12.cloned.1.call-done = f32[1024,768]{1,0:T(8,128)} async-done(((f32[1024,768]{1,0:T(8,128)}), f32[1024,768]{1,0:T(8,128)}) %all-reduce.12.cloned.1.call-update) | async-done | bytes 3145744 | tf_op jit(solution)/shard_map/psum | solution.py:68
  126.8 75.2 %all-reduce.14.cloned.1.call-done = f32[1024,768]{1,0:T(8,128)} async-done(((f32[1024,768]{1,0:T(8,128)}), f32[1024,768]{1,0:T(8,128)}) %all-reduce.14.cloned.1.call-update) | async-done | bytes 3145744 | tf_op jit(solution)/shard_map/psum | solution.py:68
  212.0 4.4 exponential_reduce_fusion
  218.7 4.7 convolution_convert_fusion.2
  227.2 75.1 %all-reduce.16.cloned.1.call-done = f32[1024,768]{1,0:T(8,128)} async-done(((f32[1024,768]{1,0:T(8,128)}), f32[1024,768]{1,0:T(8,128)}) %all-reduce.16.cloned.1.call-update) | async-done | bytes 3145744 | tf_op jit(solution)/shard_map/psum | solution.py:68
  320.9 73.6 %all-reduce.18.cloned.1.call-done = f32[1024,768]{1,0:T(8,128)} async-done(((f32[1024,768]{1,0:T(8,128)}), f32[1024,768]{1,0:T(8,128)}) %all-reduce.18.cloned.1.call-update) | async-done | bytes 3145744 | tf_op jit(solution)/shard_map/psum | solution.py:72
  398.9 5.4 convert_bitcast_fusion.1
  407.1 4.4 convolution_convert_fusion.1
  411.5 7.2 multiply_reduce_fusion.1
  418.8 7.0 multiply_convert_fusion.1
  445.9 64.0 %all-reduce.20.cloned.1.call-done = f32[1024,768]{1,0:T(8,128)} async-done(((f32[1024,768]{1,0:T(8,128)}), f32[1024,768]{1,0:T(8,128)}) %all-reduce.20.cloned.1.call-update) | async-done | bytes 3145744 | tf_op jit(solution)/shard_map/psum | solution.py:72
  560.3 8.8 copy.94
  569.1 17.0 %reshape.323 = f32[32,24576]{1,0:T(8,128)} reshape(f32[32,2,512,24]{3,2,1,0:T(8,128)} %copy.94) | data formatting | bytes 6291456 | tf_op jit(solution)/shard_map/reshape | solution.py:22
  586.1 16.3 %all-reduce.22.cloned.1.call-done = f32[1024,768]{1,0:T(8,128)} async-done(((f32[1024,768]{1,0:T(8,128)}), f32[1024,768]{1,0:T(8,128)}) %all-reduce.22.cloned.1.call-update) | async-done | bytes 3145744 | tf_op jit(solution)/shard_map/psum | solution.py:72
  602.4 4.5 multiply_reduce_fusion.5
  607.0 4.9 convert_bitcast_fusion
  618.6 7.2 multiply_reduce_fusion
  625.9 7.2 multiply_convert_fusion
  653.8 6.5 reshape.320
  691.9 11.0 %pad.4 = f32[32,111616]{1,0:T(8,128)} pad(f32[32,110688]{1,0:T(8,128)} %constant_dynamic-update-slice_fusion, f32[]{:T(128)} %constant.33.clone.1), padding=0_0x0_928 | pad | bytes 28454916 | tf_op jit(solution)/shard_map/jit(_pad)/pad | solution.py:24
  703.0 10.7 %reshape.325 = f32[27904,128]{1,0:T(8,128)} reshape(f32[32,111616]{1,0:T(8,128)} %pad.4) | data formatting | bytes 28573696 | tf_op jit(solution)/shard_map/reshape | solution.py:24
  715.5 93.2 %all-reduce.26.cloned.1.call-done = (f32[1024,768]{1,0:T(8,128)}, f32[1024,768]{1,0:T(8,128)}) async-done(((f32[1024,768]{1,0:T(8,128)}, f32[1024,768]{1,0:T(8,128)}), (f32[1024,768]{1,0:T(8,128)}, f32[1024,768]{1,0:T(8,128)})) %all-reduce.26.cloned.1.call-update) | async-done | bytes 6291472 | tf_op jit(solution)/shard_map/psum | solution.py:68
  815.4 137.2 %all-reduce.24.cloned.1.call-done = f32[27904,128]{1,0:T(8,128)} async-done(((f32[27904,128]{1,0:T(8,128)}), f32[27904,128]{1,0:T(8,128)}) %all-reduce.24.cloned.1.call-update) | async-done | bytes 14286864
  (452 shorter events, 223.7 us)
Async XLA Ops:
  7.2 105.1 %all-reduce.12.cloned.1.call-start = ((), (), s32[]{:S(2)}) async-start(), calls=%async_computation | async-start | bytes 6291456 | tf_op jit(solution)/shard_map/psum | solution.py:68
  18.1 8.5 copy-start
  33.2 168.7 %all-reduce.14.cloned.1.call-start = ((), (), s32[]{:S(2)}) async-start(), calls=%async_computation.1 | async-start | bytes 6291456 | tf_op jit(solution)/shard_map/psum | solution.py:68
  33.9 168.1 %copy-start.111 = (f32[768]{0:T(1024)}, f32[768]{0:T(1024)S(1)}, u32[]{:S(2)}) copy-start(f32[768]{0:T(1024)S(1)} %get-tuple-element.43) | copy-start | bytes 9220
  33.9 171.4 %copy-start.107 = (f32[768]{0:T(1024)}, f32[768]{0:T(1024)S(1)}, u32[]{:S(2)}) copy-start(f32[768]{0:T(1024)S(1)} %get-tuple-element.42) | copy-start | bytes 9220
  33.9 171.4 %copy-start.115 = (f32[768]{0:T(1024)}, f32[768]{0:T(1024)S(1)}, u32[]{:S(2)}) copy-start(f32[768]{0:T(1024)S(1)} %get-tuple-element.44) | copy-start | bytes 9220
  115.5 86.4 %copy-start.11 = (f32[1024,768]{1,0:T(8,128)}, f32[1024,768]{1,0:T(8,128)S(1)}, u32[]{:S(2)}) copy-start(f32[1024,768]{1,0:T(8,128)S(1)} %get-tuple-element.57) | copy-start | bytes 9437188
  115.6 86.4 %copy-start.113 = (f32[1024]{0:T(1024)}, f32[1024]{0:T(1024)S(1)}, u32[]{:S(2)}) copy-start(f32[1024]{0:T(1024)S(1)} %add_rsqrt_fusion.3) | copy-start | bytes 12292
  126.3 176.0 %all-reduce.16.cloned.1.call-start = ((), (), s32[]{:S(2)}) async-start(), calls=%async_computation.2 | async-start | bytes 6291456 | tf_op jit(solution)/shard_map/psum | solution.py:68
  224.2 78.0 %copy-start.3 = (f32[1024,768]{1,0:T(8,128)S(1)}, f32[1024,768]{1,0:T(8,128)}, u32[]{:S(2)}) copy-start(f32[1024,768]{1,0:T(8,128)} %copy-done.2) | copy-start | bytes 9437188
  226.5 168.0 %all-reduce.18.cloned.1.call-start = ((), (), s32[]{:S(2)}) async-start(), calls=%async_computation.3 | async-start | bytes 6291456 | tf_op jit(solution)/shard_map/psum | solution.py:72
  318.8 191.0 %all-reduce.20.cloned.1.call-start = ((), (), s32[]{:S(2)}) async-start(), calls=%async_computation.4 | async-start | bytes 6291456 | tf_op jit(solution)/shard_map/psum | solution.py:72
  394.5 10.6 %slice-start.3 = ((s8[12582912]{0:T(1024)(128)(4,1)}), s8[4194304]{0:T(1024)(128)(4,1)S(1)}, s32[]{:S(2)}) async-start(s8[12582912]{0:T(1024)(128)(4,1)} %bitcast.298), calls=%async_computation.11 | async-start | bytes 8388608
  398.9 7.8 slice-start.5
  434.1 168.3 %all-reduce.22.cloned.1.call-start = ((), (), s32[]{:S(2)}) async-start(), calls=%async_computation.5 | async-start | bytes 6291456 | tf_op jit(solution)/shard_map/psum | solution.py:72
  526.7 282.0 %all-reduce.26.cloned.1.call-start = ((), (), s32[]{:S(2)}) async-start(), calls=%async_computation.7 | async-start | bytes 12582912 | tf_op jit(solution)/shard_map/psum | solution.py:68
  569.1 33.3 %copy-start.12 = (f32[1024,768]{1,0:T(8,128)S(1)}, f32[1024,768]{1,0:T(8,128)}, u32[]{:S(2)}) copy-start(f32[1024,768]{1,0:T(8,128)} %copy-done.11) | copy-start | bytes 9437188
  569.1 33.3 %copy-start.112 = (f32[768]{0:T(1024)S(1)}, f32[768]{0:T(1024)}, u32[]{:S(2)}) copy-start(f32[768]{0:T(1024)} %copy-done.111) | copy-start | bytes 9220
  569.1 33.3 %copy-start.114 = (f32[1024]{0:T(1024)S(1)}, f32[1024]{0:T(1024)}, u32[]{:S(2)}) copy-start(f32[1024]{0:T(1024)} %copy-done.113) | copy-start | bytes 12292
  602.4 11.8 %slice-start = ((s8[12582912]{0:T(1024)(128)(4,1)}), s8[4194304]{0:T(1024)(128)(4,1)S(1)}, s32[]{:S(2)}) async-start(s8[12582912]{0:T(1024)(128)(4,1)} %bitcast.296), calls=%async_computation.8 | async-start | bytes 8388608
  602.4 11.8 %slice-start.1 = ((s8[12582912]{0:T(1024)(128)(4,1)}), s8[4194304]{0:T(1024)(128)(4,1)S(1)}, s32[]{:S(2)}) async-start(s8[12582912]{0:T(1024)(128)(4,1)} %bitcast.296), calls=%async_computation.9 | async-start | bytes 8388608
  671.0 7.7 copy-start.71
  681.8 270.8 %all-reduce.24.cloned.1.call-start = ((), (), s32[]{:S(2)}) async-start(), calls=%async_computation.6 | async-start | bytes 28573696
  713.7 95.1 %copy-start.18 = (f32[1024,768]{1,0:T(8,128)S(1)}, f32[1024,768]{1,0:T(8,128)}, u32[]{:S(2)}) copy-start(f32[1024,768]{1,0:T(8,128)} %copy-done.17) | copy-start | bytes 9437188
  (126 other events, 374.9 us)
Sparse Core Ops, SparseCore 0:
  33.3 78.8 all-reduce.11
  126.4 75.5 all-reduce.13
  226.6 75.5 all-reduce.15
  318.9 75.5 all-reduce.17
  434.3 75.5 all-reduce.19
  526.8 75.5 all-reduce.21
  681.9 126.8 all-reduce.25
  812.3 140.2 all-reduce.23
where the time goes:
time: 979 us; the launch traced here: 970 us
  waiting for transfers between devices  613 us (63%)
  local copies, waits for them, and re-layouts  144 us (15%)
  matrix products  118 us (12%)
  other arithmetic  75.9 us (8%)
  between operations  17.5 us (2%)
    psum x4, waiting for transfers between devices, branch_total(): return lax.psum(part, 'tensor')  322 us
    psum x3, waiting for transfers between devices, input_total(): return lax.psum(part, 'tensor')  154 us
    unnamed x9, waiting for transfers between devices  137 us
    unnamed x296, local copies, waits for them, and re-layouts  51.4 us
    dot_general x14, matrix products, outer_sum(): jnp.einsum('sa,sb->ab', left, right, preferred_element_type=jnp.float32)  28.8 us
    reshape x6, local copies, waits for them, and re-layouts, sum_packed(): lines = jnp.concatenate([b.reshape(peers, -1) for b in blocks], axis=1)  28.6 us
    dot_general x14, matrix products, back_product(): jnp.einsum('sb,ab->sa', grad, weight, preferred_element_type=jnp.float32)  23.7 us
  transfers between devices with their start and end apart: 8, of which 8 were waited for; matrix products, arithmetic and copies ran while one was open for 11% of the time, Pallas kernels for 0%

commit v1 on v0

--- a/solution.py
+++ b/solution.py
@@ -1,7 +1,582 @@
+import math
+
 import jax
 import jax.numpy as jnp
 from jax import lax
+from jax.experimental import pallas as pl
+from jax.experimental.pallas import tpu as pltpu
 from jax.sharding import PartitionSpec as P
+
+bf, f32 = jnp.bfloat16, jnp.float32
+MESH = pl.DeviceIdType.MESH
+
+CHUNKS, ROWS, D, S, T = 12, 384, 768, 1024, 256
+NB = S // T
+HALF, QUART, PIECE = ROWS // 2, ROWS // 4, ROWS // 16
+UNIT = 128 * 4
+SCALE2 = 0.125 * math.log2(math.e)
+EPS = 1e-5
+NEG = -1e30
+
+
+def nt(a, b):
+    return lax.dot_general(a, b, (((1,), (1,)), ((), ())), preferred_element_type=f32)
+
+
+def nn(a, b):
+    return lax.dot_general(a, b, (((1,), (0,)), ((), ())), preferred_element_type=f32)
+
+
+def lane(shape):
+    return lax.broadcasted_iota(jnp.int32, shape, len(shape) - 1)
+
+
+def line(shape):
+    return lax.broadcasted_iota(jnp.int32, shape, len(shape) - 2)
+
+
+def loop(count, body):
+    lax.fori_loop(0, count, lambda i, c: (body(i), c)[1], 0)
+
+
+def block(t, size=T):
+    return pl.ds(pl.multiple_of(t * size, size), size)
+
+
+def place():
+    d = lax.axis_index("dp")
+    return lax.axis_index("tensor"), d // 8, (d // 2) % 4, d % 2
+
+
+def device(x, y, z, c):
+    return (((y % 4) * 4 + (z % 4)) * 2 + c, x % 4)
+
+
+def remote(src, dst, send, recv, to):
+    return pltpu.make_async_remote_copy(
+        src_ref=src, dst_ref=dst, send_sem=send, recv_sem=recv, device_id=to, device_id_type=MESH
+    )
+
+
+def greet():
+    x, y, z, c = place()
+    bar = pltpu.get_barrier_semaphore()
+    for to in (
+        device(x + 1, y, z, c),
+        device(x + 2, y, z, c),
+        device(x + 3, y, z, c),
+        device(x, y + 1, z, c),
+        device(x, y + 3, z, c),
+        device(x, y, z + 1, c),
+        device(x, y, z + 3, c),
+        device(x, y, z, 1 - c),
+    ):
+        pl.semaphore_signal(bar, inc=1, device_id=to, device_id_type=MESH)
+    pl.semaphore_wait(bar, 8)
+
+
+class Gather:
+    SEMS = [(CHUNKS, 2, 3)] * 2 + [(CHUNKS, 2, 2)] * 4 + [(CHUNKS,)] * 2
+    BOTH = [(p, d) for p in (0, 1) for d in (0, 1)]
+
+    def __init__(self, own, full, sems):
+        self.own, self.full = own, full
+        self.xs, self.xr, self.as_, self.ar, self.bs, self.br, self.cs, self.cr = sems
+        self.at = place()
+
+    def rows(self, p, pos):
+        c = self.at[3]
+        return pl.ds(pl.multiple_of(c * HALF + p * QUART + ((pos + 4) % 4) * PIECE, 8), PIECE)
+
+    def near(self, p, step):
+        x, y, z, c = self.at
+        return device(x, y + 4 + step, z, c) if p == 0 else device(x, y, z + 4 + step, c)
+
+    def x_copy(self, ch, p, rel):
+        x, y, z, c = self.at
+        here = self.rows(p, self.at[1 + p])
+        return remote(
+            self.own.at[ch, here],
+            self.full.at[ch, rel - 1, here],
+            self.xs.at[ch, p, rel - 1],
+            self.xr.at[ch, p, rel - 1],
+            device(x + 4 - rel, y, z, c),
+        )
+
+    def a_copy(self, ch, p, d, arriving=False):
+        step = 1 - 2 * d
+        pos = self.at[1 + p] - step if arriving else self.at[1 + p]
+        ref = self.full.at[ch, :, self.rows(p, pos)]
+        return remote(ref, ref, self.as_.at[ch, p, d], self.ar.at[ch, p, d], self.near(p, step))
+
+    def b_copy(self, ch, p, d, arriving=False):
+        step = 1 - 2 * d
+        pos = self.at[1 + p] - 2 if arriving else self.at[1 + p] - step
+        ref = self.full.at[ch, :, self.rows(p, pos), pl.ds(d * (D // 2), D // 2)]
+        return remote(ref, ref, self.bs.at[ch, p, d], self.br.at[ch, p, d], self.near(p, step))
+
+    def c_copy(self, ch, arriving=False):
+        x, y, z, c = self.at
+        half = 1 - c if arriving else c
+        ref = self.full.at[ch, :, pl.ds(pl.multiple_of(half * HALF, 8), HALF)]
+        return remote(ref, ref, self.cs.at[ch], self.cr.at[ch], device(x, y, z, 1 - c))
+
+    def begin(self):
+        def send(ch):
+            for p in (0, 1):
+                for rel in (1, 3, 2):
+                    self.x_copy(ch, p, rel).start()
+
+        loop(CHUNKS, send)
+
+    def advance(self, k):
+        @pl.when(k < CHUNKS)
+        def _():
+            for p in (0, 1):
+                for rel in (1, 2, 3):
+                    self.x_copy(k, p, rel).wait_recv()
+            for p, d in self.BOTH:
+                self.a_copy(k, p, d).start()
+
+        @pl.when((k >= 1) & (k < CHUNKS + 1))
+        def _():
+            for p, d in self.BOTH:
+                self.a_copy(k - 1, p, d, True).wait_recv()
+            for p, d in self.BOTH:
+                self.b_copy(k - 1, p, d).start()
+
+        @pl.when((k >= 2) & (k < CHUNKS + 2))
+        def _():
+            for p, d in self.BOTH:
+                self.b_copy(k - 2, p, d, True).wait_recv()
+            self.c_copy(k - 2).start()
+
+    def arrive(self, ch):
+        self.c_copy(ch, True).wait_recv()
+
+    def end(self):
+        def sent(ch):
+            for p in (0, 1):
+                for rel in (1, 2, 3):
+                    self.x_copy(ch, p, rel).wait_send()
+            for p, d in self.BOTH:
+                self.a_copy(ch, p, d).wait_send()
+                self.b_copy(ch, p, d).wait_send()
+            self.c_copy(ch).wait_send()
+
+        loop(CHUNKS, sent)
+
+
+class Nowhere:
+    begin = end = lambda self: None
+    advance = arrive = lambda self, k: None
+
+
+PAIR_AT = (0, 256, 384, 512)
+THIRD_AT = (128, 192, 640, 704)
+
+
+def repack_heads(st, wb):
+    for a in range(2):
+        for r in range(4):
+            to, third = a * 768 + PAIR_AT[r], a * 768 + THIRD_AT[r]
+            wb[to : to + 128] = st[r, a * 192 : a * 192 + 128].astype(bf)
+            wb[third : third + 64] = st[r, a * 192 + 128 : a * 192 + 192].astype(bf)
+
+
+def repack_hidden(st, wb):
+    for a in range(3):
+        for r in range(4):
+            to = a * 512 + r * 128
+            wb[to : to + 128] = st[r, a * 128 : a * 128 + 128].astype(bf)
+
+
+def transpose_to(dst, src):
+    for t in range(NB):
+        dst[:, t * T : (t + 1) * T] = src[t * T : (t + 1) * T, :].T
+
+
+def rms(r):
+    return lax.rsqrt(jnp.mean(r * r, axis=-1, keepdims=True) + EPS)
+
+
+def rope(v, cs, sl, sr):
+    return v * cs + pltpu.roll(v, 96, 1) * sl + pltpu.roll(v, 32, 1) * sr
+
+
+def rope_sides(sn):
+    first = (lane(sn.shape) % 64) < 32
+    return jnp.where(first, -sn, 0.0), jnp.where(first, 0.0, sn)
+
+
+def head_lanes(h, shape):
+    at = lane(shape)
+    mine = at < 64 if h == 0 else at >= 64
+    base = 64 if h == 0 else 0
+    return mine, at - base
+
+
+def project(u, wqk, wv, cs, sn, length, qa, ka, va, v, k):
+    def step(t):
+        at = block(t)
+        ut = u[at]
+        c = cs[at]
+        sl, sr = rope_sides(sn[at])
+        shape = (T, 128)
+        bias = jnp.where(line(shape) + t * T < length, 0.0, NEG)
+        val = nt(ut, wqk[0:768])
+        for p in range(6):
+            q_p = rope(val[:, p * 128 : p * 128 + 128], c, sl, sr)
+            for h in range(2):
+                mine, side = head_lanes(h, shape)
+                qa[2 * p + h, at] = jnp.where(mine, q_p, jnp.where(side == 0, 1.0, 0.0)).astype(bf)
+        val = nt(ut, wqk[768:1536])
+        for p in range(6):
+            k_p = rope(val[:, p * 128 : p * 128 + 128], c, sl, sr)
+            k[p, at] = k_p.astype(bf)
+            for h in range(2):
+                mine, side = head_lanes(h, shape)
+                other = jnp.where(side == 0, bias, jnp.where(side < 4, -1.0, 0.0))
+                ka[2 * p + h, at] = jnp.where(mine, k_p, other).astype(bf)
+        val = nt(ut, wv[0:768])
+        for p in range(6):
+            v_p = val[:, p * 128 : p * 128 + 128]
+            v[p, at] = v_p.astype(bf)
+            for h in range(2):
+                mine, side = head_lanes(h, shape)
+                va[2 * p + h, at] = jnp.where(mine, v_p, jnp.where((side >= 1) & (side < 4), -1.0, 0.0)).astype(bf)
+
+    loop(NB, step)
+
+
+def attend(qa, ka, vt, o, ob, lse, tick):
+    def pair(p):
+        at_l = pl.ds(pl.multiple_of(p * 128, 128), 128)
+        for i in range(NB):
+            n = (i + 1) * T
+            rows = pl.ds(i * T, T)
+            diag = line((T, T)) <= lane((T, T))
+            outs, outl = [], []
+            for h in range(2):
+                s = nt(ka[2 * p + h, 0:n], qa[2 * p + h, rows])
+                tail = jnp.where(diag, s[n - T :], NEG)
+                s = tail if i == 0 else jnp.concatenate([s[: n - T], tail], axis=0)
+                m = jnp.max(s, axis=0, keepdims=True) * SCALE2
+                e = jnp.exp2(s * SCALE2 - m)
+                tot = jnp.sum(e, axis=0, keepdims=True)
+                pr = e * (1.0 / tot)
+                pb = pr.astype(bf)
+                main = nn(vt[p, h * 64 : h * 64 + 64, 0:n], pb)
+                rest = (pr - pb.astype(f32)).astype(bf)
+                outs.append(main)
+                outl.append(main + nn(vt[p, h * 64 : h * 64 + 64, 0:n], rest))
+                lse[pl.ds(p * 2 + h, 1), rows] = m + jnp.log2(tot)
+            ob[rows, at_l] = jnp.concatenate(outs, axis=0).T.astype(bf)
+            o[rows, at_l] = jnp.concatenate(outl, axis=0).T
+        tick(p)
+
+    loop(6, pair)
+
+
+def three(v):
+    hi = v.astype(bf).astype(f32)
+    mid = (v - hi).astype(bf).astype(f32)
+    low = (v - hi - mid).astype(bf).astype(f32)
+    return (hi + pltpu.roll(mid, 16, 1) + pltpu.roll(low, 32, 1)).astype(bf)
+
+
+def spread_table():
+    shape = (128, 12 * 128)
+    r, c = line(shape), lane(shape)
+    h, at = c // 128, c % 128
+    j = at - jnp.where(h % 2 == 0, 65, 1)
+    return jnp.where((j >= 0) & (j < 3) & (r == 16 * j + h), 1.0, 0.0).astype(bf)
+
+
+FWD_OUT = [
+    ((CHUNKS, 1536, D), bf),
+    ((2, 2, D, S), bf),
+    ((2, 12, S, 128), bf),
+    ((2, 12, S, 128), bf),
+    ((2, 12, S, 128), bf),
+    ((2, 6, 128, S), bf),
+    ((2, S, D), f32),
+    ((2, S, 256), bf),
+    ((2, 4, S, 512), f32),
+    ((2, 4, S, 512), f32),
+    ((2, 4, S, 128), bf),
+    ((4, S, D), f32),
+    ((S, D), f32),
+]
+FWD_VMEM = [
+    ((S, D), f32),
+    ((2, 4, ROWS, D), f32),
+    ((2, 1536, D), bf),
+    ((12, S, 128), bf),
+    ((12, S, 128), bf),
+    ((12, S, 128), bf),
+    ((6, S, 128), bf),
+    ((6, S, 128), bf),
+    ((6, 128, S), bf),
+    ((6, 128, S), bf),
+    ((S, D), f32),
+    ((S, D), bf),
+    ((128, S), f32),
+    ((S, D), bf),
+    ((2, D, S), bf),
+    ((S, D), f32),
+    ((S, D), f32),
+    ((2, 2, 512, 512), f32),
+    ((4, S, 128), bf),
+]
+
+
+def fwd_kernel(comm, length_ref, own, x_hbm, cs, sn, gains, spread, *rest):
+    if comm:
+        full, rest = rest[0], rest[1:]
+    else:
+        full, rest = spread, rest
+        spread, rest = rest[0], rest[1:]
+    outs, rest = rest[: len(FWD_OUT)], rest[len(FWD_OUT) :]
+    w_o, ut_o, qa_o, ka_o, va_o, kt_o, o_o, ob_o, a_o, b_o, hb_o, res_o, out_o = outs
+    (x, st, wb, qa, ka, va, k, v, kt, vt, o, ob, lse, u, ut, acc, res, ab, hb), rest = (
+        rest[: len(FWD_VMEM)],
+        rest[len(FWD_VMEM) :],
+    )
+    load_sem, w_sem, save_sem, ab_sem = rest[:4]
+    net = Gather(own, full, rest[4:]) if comm else Nowhere()
+    length = length_ref[0]
+
+    x_in = pltpu.make_async_copy(x_hbm, x, save_sem.at[0])
+    x_in.start()
+    if comm:
+        greet()
+    net.begin()
+    x_in.wait()
+
+    def loads(ch, slot):
+        return (
+            pltpu.make_async_copy(own.at[ch], st.at[slot, 0], load_sem.at[slot, 0]),
+            pltpu.make_async_copy(full.at[ch], st.at[slot, pl.ds(1, 3)], load_sem.at[slot, 1]),
+        )
+
+    def start_load(ch, slot):
+        net.arrive(ch)
+        for copy in loads(ch, slot):
+            copy.start()
+
+    def put_weights(ch, slot):
+        return pltpu.make_async_copy(wb.at[slot], w_o.at[ch], w_sem.at[slot])
+
+    def unpack(ch, slot, repack, first=False):
+        for copy in loads(ch, slot):
+            copy.wait()
+        if not first:
+            put_weights(ch, slot).wait()
+        repack(st.at[slot], wb.at[slot])
+        put_weights(ch, slot).start()
+
+    flying = {}
+
+    def save(name, src, dst, i):
+        flying[name] = pltpu.make_async_copy(src, dst, save_sem.at[i])
+        flying[name].start()
+
+    def settle(*names):
+        for name in names:
+            if name in flying:
+                flying.pop(name).wait()
+
+    loop(4, net.advance)
+    start_load(0, 0)
+    start_load(1, 1)
+    lse[...] = jnp.zeros((128, S), f32)
+    for layer in range(2):
+        base = layer * 6
+        settle("uta")
+        net.advance(base + 4 if layer == 0 else 11)
+
+        def enter(t):
+            at = block(t)
+            val = x[at]
+            if layer:
+                val = val * rms(val) * gains[2:3]
+            u[at] = val.astype(bf)
+
+        loop(NB, enter)
+        transpose_to(ut.at[0], u)
+        save("uta", ut.at[0], ut_o.at[layer, 0], 0)
+        unpack(base, 0, repack_heads, layer == 0)
+        unpack(base + 1, 1, repack_heads, layer == 0)
+        start_load(base + 2, 0)
+        settle("qa", "ka", "va", "kt", "o", "ob")
+        project(u, wb.at[0], wb.at[1], cs, sn, length, qa, ka, va, v, k)
+        for p in range(6):
+            transpose_to(kt.at[p], k.at[p])
+            transpose_to(vt.at[p], v.at[p])
+        save("ka", ka, ka_o.at[layer], 1)
+        save("va", va, va_o.at[layer], 2)
+        save("kt", kt, kt_o.at[layer], 3)
+        net.advance(5 if layer == 0 else 12)
+
+        def tick(p):
+            @pl.when(lax.rem(p, 2) == 1)
+            def _():
+                net.advance((6 if layer == 0 else 13) + p // 2)
+
+        attend(qa, ka, vt, o, ob, lse, tick)
+        save("o", o, o_o.at[layer], 4)
+        save("ob", ob.at[:, pl.ds(0, 256)], ob_o.at[layer], 5)
+
+        def add_lse(t):
+            at = block(t)
+            val = nn(three(lse[:, at].T), spread[...])
+            for h in range(12):
+                qa[h, at] = (qa[h, at].astype(f32) + val[:, h * 128 : h * 128 + 128]).astype(bf)
+
+        loop(NB, add_lse)
+        save("qa", qa, qa_o.at[layer], 6)
+        settle("res")
+
+        def after(t):
+            at = block(t)
+            r = x[at] + nn(ob[at], wb[1, 768:1536])
+            res[at] = r
+            n = r * rms(r)
+            if layer == 0:
+                h = n * gains[0:1]
+                acc[at] = h
+                u[at] = h.astype(bf)
+            else:
+                acc[at] = r
+                u[at] = (n * gains[3:4]).astype(bf)
+
+        loop(NB, after)
+        save("res", res, res_o.at[2 * layer if layer == 0 else 3], 7)
+        settle("utf")
+        transpose_to(ut.at[1], u)
+        save("utf", ut.at[1], ut_o.at[layer, 1], 8)
+        settle("hb")
+
+        def chunk(f):
+            ch = base + 2 + f
+            slot = lax.rem(f, 2)
+
+            @pl.when(ch + 1 < CHUNKS)
+            def _():
+                start_load(ch + 1, 1 - slot)
+
+            if layer == 0:
+
+                @pl.when(lax.rem(f, 2) == 0)
+                def _():
+                    net.advance(9 + f // 2)
+
+            unpack(ch, slot, repack_hidden)
+            w = wb.at[slot]
+
+            def step(t):
+                at = block(t, 512)
+
+                def put(j):
+                    return pltpu.make_async_copy(ab.at[t, j], (a_o, b_o)[j].at[layer, f, at], ab_sem.at[t, j])
+
+                @pl.when(f >= 1)
+                def _():
+                    put(0).wait()
+                    put(1).wait()
+
+                ub = u[at]
+                gate = nt(ub, w[0:512])
+                up = nt(ub, w[512:1024])
+                sig = 1.0 / (1.0 + jnp.exp(-gate))
+                a = gate * sig
+                hid = (a * up).astype(bf)
+                ab[t, 0] = a
+                ab[t, 1] = up * (sig + a * (1.0 - sig))
+                hb[f, at] = hid[:, 0:128]
+                acc[at] = acc[at] + nn(hid, w[1024:1536])
+                put(0).start()
+                put(1).start()
+
+            loop(2, step)
+
+        loop(4, chunk)
+        for t in range(2):
+            for j in range(2):
+                pltpu.make_async_copy(ab.at[t, j], a_o.at[layer, 0, block(0, 512)], ab_sem.at[t, j]).wait()
+        save("hb", hb, hb_o.at[layer], 9)
+        if layer == 0:
+            start_load(7, 1)
+            settle("res")
+
+            def leave(t):
+                at = block(t)
+                r = acc[at]
+                res[at] = r
+                x[at] = r * rms(r) * gains[1:2]
+
+            loop(NB, leave)
+            save("res", res, res_o.at[1], 7)
+            save("y", x, res_o.at[2], 10)
+        else:
+            settle("y")
+
+            def last(t):
+                at = block(t)
+                x[at] = jnp.where(line((T, 1)) + t * T < length, acc[at], 0.0)
+
+            loop(NB, last)
+            save("out", x, out_o, 11)
+    settle(*list(flying))
+    for slot in range(2):
+        put_weights(0, slot).wait()
+    net.end()
+
+
+def whole(memory):
+    return pl.BlockSpec(memory_space=memory)
+
+
+def forward(length, own, x, cs, sn, gains, spread, full=None):
+    comm = full is None
+    hbm, vmem = whole(pl.ANY), whole(pltpu.VMEM)
+    outs = [jax.ShapeDtypeStruct(s, d) for s, d in FWD_OUT]
+    if comm:
+        outs = [jax.ShapeDtypeStruct((CHUNKS, 3, ROWS, D), f32)] + outs
+    dma = pltpu.SemaphoreType.DMA
+    result = pl.pallas_call(
+        lambda *refs: fwd_kernel(comm, *refs),
+        out_shape=outs,
+        in_specs=[whole(pltpu.SMEM), hbm, hbm, vmem, vmem, vmem] + ([] if comm else [hbm]) + [vmem],
+        out_specs=[hbm] * len(outs),
+        scratch_shapes=[pltpu.VMEM(s, d) for s, d in FWD_VMEM]
+        + [dma((2, 2)), dma((2,)), dma((12,)), dma((2, 2))]
+        + ([dma(s) for s in Gather.SEMS] if comm else []),
+        compiler_params=pltpu.CompilerParams(
+            vmem_limit_bytes=62 * 2**20,
+            **(dict(collective_id=0, has_side_effects=True) if comm else {}),
+        ),
+    )(length, own, x, cs, sn, gains, *([] if comm else [full]), spread)
+    return result[1:] if comm else result
+
+
+def pack_own(wq, wk, wv, wo, wg, wu, wd):
+    parts = []
+    for layer in range(2):
+        parts += [wq[layer].T, wk[layer].T, wv[layer].T, wo[layer]]
+        gate, up, down = wg[layer].T, wu[layer].T, wd[layer]
+        for f in range(4):
+            part = slice(f * 128, f * 128 + 128)
+            parts += [gate[part], up[part], down[part]]
+    return jnp.concatenate(parts).astype(f32).reshape(CHUNKS, ROWS, D)
+
+
+def rope_tables(count):
+    freq = 10000.0 ** (-jnp.arange(32, dtype=f32) * 2.0 / 64)
+    angle = jnp.arange(count, dtype=f32)[:, None] * freq[None, :]
+    cosine, sine = jnp.cos(angle), jnp.sin(angle)
+    return jnp.concatenate([cosine] * 4, axis=1), jnp.concatenate([sine] * 4, axis=1)
 
 HEAD_DIM = 64
 
@@ -30,7 +605,7 @@
     return tuple(finished)
 
 
-def rope_tables(count):
+def rope_tables0(count):
     half = HEAD_DIM // 2
     freq = 10000.0 ** (-jnp.arange(half, dtype=jnp.float32) * 2.0 / HEAD_DIM)
     angle = jnp.arange(count, dtype=jnp.float32)[:, None] * freq[None, :]
@@ -178,7 +753,7 @@
 ):
     count = block_input.shape[0]
     length = lengths[0]
-    cosine, sine = rope_tables(count)
+    cosine, sine = rope_tables0(count)
     live = (jnp.arange(count, dtype=jnp.int32) < length).astype(jnp.float32)[:, None]
     part, attn0 = attend_forward(
         block_input.astype(jnp.bfloat16),
@@ -244,6 +819,9 @@
     summed = [total[index] for index in range(7)]
     gain_grads = total[7][:3]
     ffn_gain_grad = total[7][3]
+    cs, sn = rope_tables(count)
+    kept = forward(lengths, pack_own(w_query, w_key, w_value, w_output, w_gate, w_up, w_down), block_input, cs, sn, gains, spread_table())
+    block_output = kept[12]
     return (
         block_output,
         input_grad,

time: 979 us -> 958 us (0.979)
  waiting for transfers between devices: 613 us -> 368 us
  Pallas kernels: 0 us -> 189 us
  local copies, waits for them, and re-layouts: 144 us -> 168 us
  starting transfers between devices: 1.18 us -> 12.5 us
  other arithmetic: 75.9 us -> 86.6 us
  matrix products: 118 us -> 108 us
    pallas_call x0 -> x1, Pallas kernels: none -> 189 us  [forward(): pl.pallas_call(lambda *refs: fwd_kernel(comm, *refs), out_shape=outs, in_...]
    unnamed x9, waiting for transfers between devices: 137 us -> 0.13 us
    psum x4 -> x3, waiting for transfers between devices: 322 us -> 218 us  [branch_total(): return lax.psum(part, 'tensor')]
    slice x4 -> x22, local copies, waits for them, and re-layouts: 4.81 us -> 23.3 us  [the longest x18 18.4 us: pack_own(): parts += [gate[part], up[part], down[part]]]
    psum x4 -> x3, starting transfers between devices: 0.63 us -> 11.5 us  [branch_total(): return lax.psum(part, 'tensor')]
    psum x3 -> x4, waiting for transfers between devices: 154 us -> 149 us  [input_total(): return lax.psum(part, 'tensor')]
    unnamed x296 -> x372, local copies, waits for them, and re-layouts: 51.4 us -> 55.4 us
  transfers between devices with their start and end apart: 8 -> 8, of which waited for: 8 -> 6; matrix products, arithmetic and copies ran while one was open for 11% -> 17% of each run, Pallas kernels for 0% -> 20%
where the time goes in v1:
time: 958 us; the launch traced here: 949 us
  waiting for transfers between devices  368 us (38%)
  Pallas kernels  189 us (20%)
  local copies, waits for them, and re-layouts  168 us (18%)
  matrix products  108 us (11%)
  other arithmetic  86.6 us (9%)
  between operations  17.8 us (2%)
  starting transfers between devices  12.5 us (1%)
    psum x3, waiting for transfers between devices, branch_total(): return lax.psum(part, 'tensor')  218 us
    pallas_call x1, Pallas kernels, forward(): pl.pallas_call(lambda *refs: fwd_kernel(comm, *refs), out_shape=outs, in_...  189 us
    psum x4, waiting for transfers between devices, input_total(): return lax.psum(part, 'tensor')  149 us
    unnamed x372, local copies, waits for them, and re-layouts  55.4 us
    reshape x6, local copies, waits for them, and re-layouts, sum_packed(): lines = jnp.concatenate([b.reshape(peers, -1) for b in blocks], axis=1)  27.8 us
    dot_general x14, matrix products, outer_sum(): jnp.einsum('sa,sb->ab', left, right, preferred_element_type=jnp.float32)  26.6 us
    dot_general x14, matrix products, back_product(): jnp.einsum('sb,ab->sa', grad, weight, preferred_element_type=jnp.float32)  19.3 us
  transfers between devices with their start and end apart: 8, of which 6 were waited for; matrix products, arithmetic and copies ran while one was open for 17% of the time, Pallas kernels for 20%

profile of v1, /device:TPU:1, one launch (start us, length us, event | category | flops | bytes accessed | tf_op | source)
XLA Modules:
  0.0 949.0 jit_solution(2763060858658244322)
XLA Ops:
  30.2 4.7 convolution_convert_fusion.3
  38.0 11.4 %all-reduce.13.cloned.1.call-start = ((), (), s32[]{:S(2)}) async-start(), calls=%async_computation.1 | async-start | bytes 6291456 | tf_op jit(solution)/shard_map/psum | solution.py:643
  50.1 67.0 %all-reduce.11.cloned.1.call-done = f32[1024,768]{1,0:T(8,128)} async-done(((f32[1024,768]{1,0:T(8,128)}), f32[1024,768]{1,0:T(8,128)}) %all-reduce.11.cloned.1.call-update) | async-done | bytes 3145744 | tf_op jit(solution)/shard_map/psum | solution.py:643
  131.1 75.7 %all-reduce.13.cloned.1.call-done = f32[1024,768]{1,0:T(8,128)} async-done(((f32[1024,768]{1,0:T(8,128)}), f32[1024,768]{1,0:T(8,128)}) %all-reduce.13.cloned.1.call-update) | async-done | bytes 3145744 | tf_op jit(solution)/shard_map/psum | solution.py:643
  222.8 4.7 convolution_convert_fusion.2
  230.6 75.7 %all-reduce.15.cloned.1.call-done = f32[1024,768]{1,0:T(8,128)} async-done(((f32[1024,768]{1,0:T(8,128)}), f32[1024,768]{1,0:T(8,128)}) %all-reduce.15.cloned.1.call-update) | async-done | bytes 3145744 | tf_op jit(solution)/shard_map/psum | solution.py:643
  329.3 69.5 %all-reduce.17.cloned.1.call-done = f32[1024,768]{1,0:T(8,128)} async-done(((f32[1024,768]{1,0:T(8,128)}), f32[1024,768]{1,0:T(8,128)}) %all-reduce.17.cloned.1.call-update) | async-done | bytes 3145744 | tf_op jit(solution)/shard_map/psum | solution.py:647
  403.2 5.5 convert_bitcast_fusion.1
  411.5 7.1 multiply_reduce_fusion.1
  423.1 7.0 multiply_convert_fusion.1
  453.8 60.4 %all-reduce.19.cloned.1.call-done = f32[1024,768]{1,0:T(8,128)} async-done(((f32[1024,768]{1,0:T(8,128)}), f32[1024,768]{1,0:T(8,128)}) %all-reduce.19.cloned.1.call-update) | async-done | bytes 3145744 | tf_op jit(solution)/shard_map/psum | solution.py:647
  531.9 5.5 fusion.45
  559.9 8.8 copy.206
  568.7 17.3 %reshape.335 = f32[32,24576]{1,0:T(8,128)} reshape(f32[32,2,512,24]{3,2,1,0:T(8,128)} %copy.206) | data formatting | bytes 6291456 | tf_op jit(solution)/shard_map/reshape | solution.py:597
  587.4 19.5 %all-reduce.21.cloned.1.call-done = f32[1024,768]{1,0:T(8,128)} async-done(((f32[1024,768]{1,0:T(8,128)}), f32[1024,768]{1,0:T(8,128)}) %all-reduce.21.cloned.1.call-update) | async-done | bytes 3145744 | tf_op jit(solution)/shard_map/psum | solution.py:647
  611.5 4.9 convert_bitcast_fusion
  618.8 7.2 multiply_reduce_fusion
  629.7 7.2 multiply_convert_fusion
  663.9 6.5 reshape.332
  682.3 11.1 %pad.4 = f32[32,111616]{1,0:T(8,128)} pad(f32[32,110688]{1,0:T(8,128)} %constant_dynamic-update-slice_fusion.16, f32[]{:T(128)} %constant.81.clone.1), padding=0_0x0_928 | pad | bytes 28454916 | tf_op jit(solution)/shard_map/jit(_pad)/pad | solution.py:599
  693.3 11.4 %reshape.337 = f32[27904,128]{1,0:T(8,128)} reshape(f32[32,111616]{1,0:T(8,128)} %pad.4) | data formatting | bytes 28573696 | tf_op jit(solution)/shard_map/reshape | solution.py:599
  724.7 6.4 convert.1.refs_1_
  733.9 188.6 %shard_map.194 = (f32[12,3,384,768]{3,2,1,0:T(8,128)}, bf16[12,1536,768]{2,1,0:T(8,128)(2,1)}, bf16[2,2,768,1024]{3,2,1,0:T(8,128)(2,1)}, bf16[2,12,1024,128]{3,...) custom-call(s32[1]{0:T(128)} %copy.277.refs_0_, ...), custom_call_target="tpu_custom_call" | custom-call | tf_op jit(solution)/shard_map/pallas_call | solution.py:548
  923.8 4.9 add.195
  (557 shorter events, 243.2 us)
Async XLA Ops:
  7.2 109.9 %all-reduce.11.cloned.1.call-start = ((), (), s32[]{:S(2)}) async-start(), calls=%async_computation | async-start | bytes 6291456 | tf_op jit(solution)/shard_map/psum | solution.py:643
  35.7 13.8 %copy-start.145 = (f32[4,768]{1,0:T(4,128)S(1)}, f32[4,768]{1,0:T(4,128)}, u32[]{:S(2)}) copy-start(f32[4,768]{1,0:T(4,128)} %refs_5_.1) | copy-start | bytes 36868
  38.0 168.7 %all-reduce.13.cloned.1.call-start = ((), (), s32[]{:S(2)}) async-start(), calls=%async_computation.1 | async-start | bytes 6291456 | tf_op jit(solution)/shard_map/psum | solution.py:643
  50.1 156.6 %copy-start.131 = (f32[768]{0:T(1024)}, f32[768]{0:T(1024)S(1)}, u32[]{:S(2)}) copy-start(f32[768]{0:T(1024)S(1)} %get-tuple-element.56) | copy-start | bytes 9220
  50.1 160.0 %copy-start.127 = (f32[768]{0:T(1024)}, f32[768]{0:T(1024)S(1)}, u32[]{:S(2)}) copy-start(f32[768]{0:T(1024)S(1)} %get-tuple-element.55) | copy-start | bytes 9220
  50.1 160.0 %copy-start.135 = (f32[768]{0:T(1024)}, f32[768]{0:T(1024)S(1)}, u32[]{:S(2)}) copy-start(f32[768]{0:T(1024)S(1)} %get-tuple-element.57) | copy-start | bytes 9220
  120.4 86.3 %copy-start.8 = (f32[1024,768]{1,0:T(8,128)}, f32[1024,768]{1,0:T(8,128)S(1)}, u32[]{:S(2)}) copy-start(f32[1024,768]{1,0:T(8,128)S(1)} %get-tuple-element.68) | copy-start | bytes 9437188
  120.4 86.3 %copy-start.133 = (f32[1024]{0:T(1024)}, f32[1024]{0:T(1024)S(1)}, u32[]{:S(2)}) copy-start(f32[1024]{0:T(1024)S(1)} %add_rsqrt_fusion.3) | copy-start | bytes 12292
  131.0 175.2 %all-reduce.15.cloned.1.call-start = ((), (), s32[]{:S(2)}) async-start(), calls=%async_computation.2 | async-start | bytes 6291456 | tf_op jit(solution)/shard_map/psum | solution.py:643
  228.3 78.0 %copy-start.3 = (f32[1024,768]{1,0:T(8,128)S(1)}, f32[1024,768]{1,0:T(8,128)}, u32[]{:S(2)}) copy-start(f32[1024,768]{1,0:T(8,128)} %copy-done.2) | copy-start | bytes 9437188
  230.5 168.3 %all-reduce.17.cloned.1.call-start = ((), (), s32[]{:S(2)}) async-start(), calls=%async_computation.3 | async-start | bytes 6291456 | tf_op jit(solution)/shard_map/psum | solution.py:647
  323.1 191.1 %all-reduce.19.cloned.1.call-start = ((), (), s32[]{:S(2)}) async-start(), calls=%async_computation.4 | async-start | bytes 6291456 | tf_op jit(solution)/shard_map/psum | solution.py:647
  438.5 168.4 %all-reduce.21.cloned.1.call-start = ((), (), s32[]{:S(2)}) async-start(), calls=%async_computation.5 | async-start | bytes 6291456 | tf_op jit(solution)/shard_map/psum | solution.py:647
  531.2 392.5 %all-reduce.23.cloned.1.call-start = ((), (), s32[]{:S(2)}) async-start(), calls=%async_computation.6 | async-start | bytes 6291456 | tf_op jit(solution)/shard_map/psum | solution.py:647
  568.7 17.4 %copy-start.148 = (f32[768]{0:T(1024)S(1)}, f32[768]{0:T(1024)}, u32[]{:S(2)}) copy-start(f32[768]{0:T(1024)} %get-tuple-element.48) | copy-start | bytes 9220
  568.7 18.1 %copy-start.146 = (f32[768]{0:T(1024)S(1)}, f32[768]{0:T(1024)}, u32[]{:S(2)}) copy-start(f32[768]{0:T(1024)} %get-tuple-element.50) | copy-start | bytes 9220
  568.7 38.3 %copy-start.9 = (f32[1024,768]{1,0:T(8,128)S(1)}, f32[1024,768]{1,0:T(8,128)}, u32[]{:S(2)}) copy-start(f32[1024,768]{1,0:T(8,128)} %copy-done.8) | copy-start | bytes 9437188
  568.7 38.3 %copy-start.132 = (f32[768]{0:T(1024)S(1)}, f32[768]{0:T(1024)}, u32[]{:S(2)}) copy-start(f32[768]{0:T(1024)} %copy-done.131) | copy-start | bytes 9220
  568.7 38.3 %copy-start.134 = (f32[1024]{0:T(1024)S(1)}, f32[1024]{0:T(1024)}, u32[]{:S(2)}) copy-start(f32[1024]{0:T(1024)} %copy-done.133) | copy-start | bytes 12292
  648.8 279.9 %all-reduce.25.cloned.1.call-start = ((), (), s32[]{:S(2)}) async-start(), calls=%async_computation.7 | async-start | bytes 28573696
  706.2 14.0 %copy-start.100 = (bf16[128,768]{0,1:T(8,128)(2,1)S(1)}, bf16[128,768]{0,1:T(8,128)(2,1)}, u32[]{:S(2)}) copy-start(bf16[128,768]{0,1:T(8,128)(2,1)} %get-tuple-element.105) | copy-start | bytes 589828
  707.4 14.1 %copy-start.99 = (bf16[128,768]{0,1:T(8,128)(2,1)S(1)}, bf16[128,768]{0,1:T(8,128)(2,1)}, u32[]{:S(2)}) copy-start(bf16[128,768]{0,1:T(8,128)(2,1)} %get-tuple-element.104) | copy-start | bytes 589828
  707.4 14.4 %copy-start.38 = (bf16[2,768,192]{1,2,0:T(8,128)(2,1)S(1)}, bf16[2,768,192]{1,2,0:T(8,128)(2,1)}, u32[]{:S(2)}) copy-start(bf16[2,768,192]{1,2,0:T(8,128)(2,1)} %param.14) | copy-start | bytes 1769476
  733.9 188.6 %copy-start.152 = (u32[128]{0:T(128)S(1)}, u32[128]{0:T(128)}, u32[]{:S(2)}) copy-start(u32[128]{0:T(128)} %constant.92) | copy-start | bytes 1540
  (148 other events, 526.3 us)
Sparse Core Ops, SparseCore 0:
  38.2 78.9 all-reduce.10
  131.1 75.5 all-reduce.12
  230.7 75.5 all-reduce.14
  323.2 75.5 all-reduce.16
  438.6 75.5 all-reduce.18
  531.4 75.5 all-reduce.20
  648.9 75.5 all-reduce.22
  728.0 193.5 all-reduce.24
